TPU v7x, 32 devices: a whole 2x2x4 slice. The times are simulated.
32 devices in a mesh: box: 8 (over z, y), dir: 4 (over x, core).
Axes of the slice: x: 2, y: 2, z: 4, core: 2. Of those that a mesh axis runs over, the one named last changes fastest.
Arguments:
- pattern: float32 [512, 8, 4096], P('dir', None, 'box'), may hold values from -6 to 6
- child_coef: float32 [2, 4, 512], P(None, None, 'dir'), may hold values from -3 to 3
- child_mask: int32 [4, 4096], P(None, 'box'), may hold values 0 or 1
- interp_index: int32 [16, 2048], replicated, may hold values from 0 to 511, as said below
- interp_weight: float32 [16, 2048], replicated, may hold values from -1.25 to 1.25
- phase_angle: float32 [8, 2048], replicated, may hold values from -3.140625 to 3.140625
- parent_coef: float32 [2, 32, 2048], replicated, may hold values from -3 to 3
- parent_mask: int32 [32, 512], replicated, may hold values 0 or 1
Outputs:
- local_field: float32 [512, 8, 4096], P('dir', None, 'box')
Inputs may be any that keep to these rules, and one draw needn't show every extreme that they name: `interp_index`: child directions form a grid of 16 polar by 32 azimuthal angles, numbered as (azimuth % 4) * 128 + polar * 8 + azimuth // 4; each parent direction reads the 16 child directions of a 4 by 4 block of neighbouring angles, the azimuth wrapping round.
All inputs are finite; a program needn't handle non-finite values. No bound on the sum of `child_mask` on one device may be relied on, other than what follows from the above.
Results may differ from a plain program's by a relative error of at most 0.000053.
Values sent between devices are 32-bit elements; how exact they have to be, the bound alone decides.
A program may use at most 192 MiB of HBM per device.

v0:
```python
import functools

import jax
import jax.numpy as jnp
from jax import lax
from jax.experimental import pallas as pl
from jax.experimental.pallas import tpu as pltpu
from jax.sharding import PartitionSpec as P

F32, BF16 = jnp.float32, jnp.bfloat16
VMEM_LIMIT = 56 * 1024 * 1024


def split(x):
    hi = x.astype(BF16)
    return hi, (x - hi.astype(F32)).astype(BF16)


def turn(x):
    half = x.shape[1] // 2
    return jnp.concatenate([-x[:, half:], x[:, :half]], axis=1)


def nn(a, b):
    return lax.dot_general(a, b, (((1,), (0,)), ((), ())), preferred_element_type=F32)


def nt(a, b):
    return lax.dot_general(a, b, (((1,), (1,)), ((), ())), preferred_element_type=F32)


def build_weights(first, idx, wgt, cos, sin, whi, wlo):
    points, p = idx.shape
    group = cos.shape[0]
    q = whi.shape[0] // (2 * group)
    rows = first + lax.broadcasted_iota(jnp.int32, (q, p), 0)
    m = jnp.zeros((q, p), F32)
    for k in range(points):
        m = m + jnp.where(rows == idx[k : k + 1, :], wgt[k : k + 1, :], F32(0.0))
    for part, table in enumerate((cos, sin)):
        for g in range(group):
            hi, lo = split(m * table[g : g + 1, :])
            at = (part * group + g) * q
            whi[at : at + q, :] = hi
            wlo[at : at + q, :] = lo


def up_kernel(idx, wgt, cos, sin, pat, out, xhi, xlo, whi, wlo):
    q = pat.shape[2]
    group = cos.shape[0]
    s_count = pat.shape[0] // group
    rows = s_count * pat.shape[1]

    @pl.when(pl.program_id(0) == 0)
    def _():
        for g in range(group):
            x = pat[...].reshape(s_count, group, pat.shape[1], q)[:, g]
            for part, y in enumerate((x, turn(x))):
                hi, lo = split(y.reshape(rows, q))
                at = (part * group + g) * q
                xhi[:, at : at + q] = hi
                xlo[:, at : at + q] = lo

    first = lax.axis_index("dir") * q
    build_weights(first, idx[...], wgt[...], cos[...], sin[...], whi, wlo)
    total = nn(xhi[...], whi[...]) + nn(xhi[...], wlo[...]) + nn(xlo[...], whi[...])
    out[...] = total.reshape(s_count, pat.shape[1], -1)


def translate_kernel(field, coef, mask, out, *, reach):
    count = out.shape[0]
    offsets = list(range(-reach, 0)) + list(range(1, reach + 1))
    block = 4

    def step(i, _):
        s0 = i * block
        for lane in range(0, out.shape[2], 128):
            real = [jnp.zeros((out.shape[1], 128), F32) for _ in range(block)]
            imag = [jnp.zeros((out.shape[1], 128), F32) for _ in range(block)]
            for k, t in enumerate(offsets):
                cr = coef[0, k : k + 1, lane : lane + 128]
                ci = coef[1, k : k + 1, lane : lane + 128]
                for j in range(block):
                    f = field[s0 + j + reach + t, :, lane : lane + 128] * mask[k, s0 + j]
                    real[j] = real[j] + f * cr
                    imag[j] = imag[j] + f * ci
            for j in range(block):
                half = out.shape[1] // 2
                b = imag[j]
                out[s0 + j, :, lane : lane + 128] = real[j] + jnp.concatenate([-b[half:], b[:half]], axis=0)
        return 0

    lax.fori_loop(0, count // block, step, 0)


def down_kernel(idx, wgt, cos, sin, loc, child, out, acc, whi, wlo):
    group = cos.shape[0]
    s_count, comps, p = loc.shape
    q = out.shape[2]
    step = pl.program_id(0)
    first = lax.axis_index("dir") * q
    build_weights(first, idx[...], wgt[...], cos[...], sin[...], whi, wlo)
    x = loc[...]
    n = group * q
    total = None
    for part, y in enumerate((x, -turn(x))):
        hi, lo = split(y.reshape(s_count * comps, p))
        wh, wl = whi[part * n : (part + 1) * n, :], wlo[part * n : (part + 1) * n, :]
        for term in (nt(hi, wh), nt(hi, wl), nt(lo, wh)):
            total = term if total is None else total + term

    @pl.when(step == 0)
    def _():
        acc[...] = total

    @pl.when(step > 0)
    def _():
        acc[...] = acc[...] + total

    @pl.when(step == pl.num_programs(0) - 1)
    def _():
        for g in range(group):
            def put(s, _):
                at = pl.ds(pl.multiple_of(s * comps, comps), comps)
                out[s * group + g] = acc[at, g * q : (g + 1) * q] + child[s * group + g]
                return 0
            lax.fori_loop(0, s_count, put, 0)


def halo(block, width):
    count = lax.axis_size("box")
    forward = [(i, i + 1) for i in range(count - 1)]
    backward = [(b, a) for a, b in forward]
    low = lax.ppermute(block[-width:], "box", forward)
    high = lax.ppermute(block[:width], "box", backward)
    return jnp.concatenate([low, block, high], axis=0)


def body(pattern, child_coef, child_mask, interp_index, interp_weight, phase_angle, parent_coef, parent_mask):
    q, comps, boxes = pattern.shape
    p_all = interp_index.shape[1]
    group = phase_angle.shape[0]
    s_count = boxes // group
    dir_size = lax.axis_size("dir")
    p_own = p_all // dir_size
    dir_rank = lax.axis_index("dir")
    box_rank = lax.axis_index("box")
    cos, sin = jnp.cos(phase_angle), jnp.sin(phase_angle)
    pat = jnp.transpose(pattern, (2, 1, 0))
    chunk = 256
    col = lambda rows: pl.BlockSpec((rows, chunk), lambda i: (0, i))
    params = pltpu.CompilerParams(vmem_limit_bytes=VMEM_LIMIT)
    wsize = 2 * group * q
    rows = s_count * comps
    whole = lambda shape: pl.BlockSpec(shape, lambda i: (0,) * len(shape))
    field = pl.pallas_call(
        up_kernel,
        grid=(p_all // chunk,),
        out_shape=jax.ShapeDtypeStruct((s_count, comps, p_all), F32),
        in_specs=[col(interp_index.shape[0]), col(interp_index.shape[0]), col(group), col(group), whole(pat.shape)],
        out_specs=pl.BlockSpec((s_count, comps, chunk), lambda i: (0, 0, i)),
        scratch_shapes=[pltpu.VMEM((rows, wsize), BF16)] * 2 + [pltpu.VMEM((wsize, chunk), BF16)] * 2,
        compiler_params=params,
    )(interp_index, interp_weight, cos, sin, pat)
    field = lax.psum_scatter(field, "dir", scatter_dimension=2, tiled=True)

    def translate(x, coef, mask, reach):
        return pl.pallas_call(
            functools.partial(translate_kernel, reach=reach),
            out_shape=jax.ShapeDtypeStruct((x.shape[0] - 2 * reach,) + x.shape[1:], F32),
            in_specs=[
                pl.BlockSpec(memory_space=pltpu.VMEM),
                pl.BlockSpec(memory_space=pltpu.VMEM),
                pl.BlockSpec(memory_space=pltpu.SMEM),
            ],
            compiler_params=params,
        )(x, coef, mask.astype(F32))

    child_reach = child_coef.shape[1] // 2
    child = translate(halo(pat, child_reach), child_coef, child_mask, child_reach)
    reach = parent_coef.shape[1] // 2
    own_coef = lax.dynamic_slice_in_dim(parent_coef, dir_rank * p_own, p_own, 2)
    own_mask = lax.dynamic_slice_in_dim(parent_mask, box_rank * s_count, s_count, 1)
    local = translate(halo(field, reach), own_coef, own_mask, reach)
    local = lax.all_gather(local, "dir", axis=2, tiled=True)
    out = pl.pallas_call(
        down_kernel,
        grid=(p_all // chunk,),
        out_shape=jax.ShapeDtypeStruct((boxes, comps, q), F32),
        in_specs=[
            col(interp_index.shape[0]), col(interp_index.shape[0]), col(group), col(group),
            pl.BlockSpec((s_count, comps, chunk), lambda i: (0, 0, i)),
            whole(pat.shape),
        ],
        out_specs=whole(pat.shape),
        scratch_shapes=[pltpu.VMEM((rows, group * q), F32)] + [pltpu.VMEM((wsize, chunk), BF16)] * 2,
        compiler_params=params,
    )(interp_index, interp_weight, cos, sin, local, child)
    return jnp.transpose(out, (2, 1, 0))


def solution(mesh):
    placed = (P("dir", None, "box"), P(None, None, "dir"), P(None, "box"), P(), P(), P(), P(), P())
    return jax.shard_map(
        body, mesh=mesh, in_specs=placed, out_specs=P("dir", None, "box"), check_vma=False
    )
```

profile of v0, /device:TPU:0, one launch (start us, length us, event | category | flops | bytes accessed | tf_op | source)
XLA Modules:
  0.0 177.6 jit_solution(694081097974453142)
XLA Ops:
  6.5 0.0 copy-start
  6.5 0.0 copy-start.2
  6.5 0.0 reduce-scatter.2.cloned.1.call-start
  6.5 3.2 %copy.9 = f32[128,8,512]{0,1,2:T(8,128)} copy(f32[128,8,512]{2,1,0:T(8,128)} %param.8) | data formatting | bytes 4194304 | tf_op args[0]
  9.7 0.0 copy-done.2
  9.7 0.9 fusion.2
  10.6 20.3 %shard_map.82 = f32[64,8,2048]{2,1,0:T(8,128)} custom-call(s32[16,2048]{1,0:T(8,128)} %idx.3, f32[16,2048]{1,0:T(8,128)} %wgt.3, f32[8,2048]{1,0:T(8,128)} %get-tuple-element.10.cos, f32[8,2048]{1,0:T(8,128)} %get-tuple-element.9.sin, f32[512,8,128]{2,1,0:T(8,128)} %bitcast.2), custom_call_target="tpu_custom_call" | custom-call | tf_op jit(solution)/shard_map/pallas_call | solution.py:156
  30.9 0.0 reduce-scatter.2.cloned.1.call-update
  31.0 0.0 all-gather.2.cloned.1.call-start
  31.0 47.3 %reduce-scatter.2.cloned.1.call-done = f32[64,8,512]{2,1,0:T(8,128)} async-done(((f32[64,8,2048]{2,1,0:T(8,128)}), f32[64,8,512]{2,1,0:T(8,128)}) %reduce-scatter.2.cloned.1.call-update) | async-done | bytes 1048592 | tf_op jit(solution)/shard_map/reduce_scatter | solution.py:165
  78.3 1.1 fusion.1
  79.4 3.4 %collective-permute-start = (f32[16,8,512]{2,1,0:T(8,128)S(1)}, f32[16,8,512]{2,1,0:T(8,128)S(1)}, u32[]{:S(2)}, u32[]{:S(2)}) collective-permute-start(f32[16,8,512]{2,1,0:T(8,128)S(1)} %get-tuple-element.7), channel_id=1, source_target_pairs={{0,4},{4,8},{8,12},{12,16},{16,20},{20,24},{24,28},{1,5},{5,9},{9,... | collective-permute-start | bytes 786440 | tf_op jit(solution)/shard_map/ppermute | solution.py:134
  82.8 1.3 collective-permute-start.1
  84.1 1.4 dynamic-slice_convert_fusion.mask
  85.5 0.0 copy-done
  85.5 0.7 constant_dynamic-slice_fusion.coef
  86.2 7.8 %collective-permute-done = f32[16,8,512]{2,1,0:T(8,128)S(1)} collective-permute-done((f32[16,8,512]{2,1,0:T(8,128)S(1)}, f32[16,8,512]{2,1,0:T(8,128)S(1)}, u32[]{:S(2)}, u32[]{:S(2)}) %collective-permute-start) | collective-permute-done | bytes 262176 | tf_op jit(solution)/shard_map/ppermute | solution.py:134
  93.9 0.0 collective-permute-done.1
  93.9 2.5 %pad_maximum_fusion.1.field = f32[96,8,512]{2,1,0:T(8,128)} fusion(f32[16,8,512]{2,1,0:T(8,128)S(1)} %collective-permute-done.1, f32[64,8,512]{2,1,0:T(8,128)} %reduce-scatter.2.cloned.1.call-done, f32[16,8,512]{2,1,0:T(8,128)S(1)} %collective-permute-done), kind=kLoop, calls=%fused_computation.1 | loop fusion | flops 786432 | bytes 3145728 | tf_op jit(solution)/shard_map/concatenate | solution.py:136
  96.5 0.0 copy-start.1
  96.5 0.0 copy-start.3
  96.5 10.4 %shard_map.83 = f32[64,8,512]{2,1,0:T(8,128)} custom-call(f32[96,8,512]{2,1,0:T(8,128)} %pad_maximum_fusion.1.field, f32[2,32,512]{2,1,0:T(8,128)} %constant_dynamic-slice_fusion.coef, f32[32,64]{1,0:T(8,128)} %dynamic-slice_convert_fusion.mask), custom_call_target="tpu_custom_call" | custom-call | tf_op jit(solution)/shard_map/pallas_call | solution.py:168
  106.9 0.0 all-gather.2.cloned.1.call-update
  106.9 0.0 copy-done.1
  106.9 4.4 %collective-permute-start.2 = (f32[2,8,128]{2,1,0:T(8,128)S(1)}, f32[2,8,128]{2,1,0:T(8,128)S(1)}, u32[]{:S(2)}, u32[]{:S(2)}) collective-permute-start(f32[2,8,128]{2,1,0:T(8,128)S(1)} %get-tuple-element.5), channel_id=1, source_target_pairs={{0,4},{4,8},{8,12},{12,16},{16,20},{20,24},{24,28},{1,5},{5,9},{9,... | collective-permute-start | bytes 24584 | tf_op jit(solution)/shard_map/ppermute | solution.py:134
  111.3 1.3 collective-permute-start.3
  112.6 0.0 copy-done.3
  112.7 0.6 convert_element_type.7.mask
  113.2 0.0 collective-permute-done.2
  113.3 4.0 %collective-permute-done.3 = f32[2,8,128]{2,1,0:T(8,128)S(1)} collective-permute-done((f32[2,8,128]{2,1,0:T(8,128)S(1)}, f32[2,8,128]{2,1,0:T(8,128)S(1)}, u32[]{:S(2)}, u32[]{:S(2)}) %collective-permute-start.3) | collective-permute-done | bytes 8224 | tf_op jit(solution)/shard_map/ppermute | solution.py:135
  117.3 1.5 pad_maximum_fusion.field
  118.7 6.8 %shard_map.84.child = f32[512,8,128]{2,1,0:T(8,128)} custom-call(f32[516,8,128]{2,1,0:T(8,128)} %pad_maximum_fusion.field, f32[2,4,128]{2,1,0:T(4,128)} %coef.1, f32[4,512]{1,0:T(4,128)} %convert_element_type.7.mask), custom_call_target="tpu_custom_call" | custom-call | tf_op jit(solution)/shard_map/pallas_call | solution.py:168
  125.5 17.1 %all-gather.2.cloned.1.call-done.loc = f32[64,8,2048]{2,1,0:T(8,128)} async-done(((f32[64,8,512]{2,1,0:T(8,128)}), f32[64,8,2048]{2,1,0:T(8,128)}) %all-gather.2.cloned.1.call-update) | async-done | bytes 4194320 | tf_op jit(solution)/shard_map/all_gather | solution.py:185
  142.6 25.1 %shard_map.85 = f32[512,8,128]{2,1,0:T(8,128)} custom-call(s32[16,2048]{1,0:T(8,128)} %idx.3, f32[16,2048]{1,0:T(8,128)} %wgt.3, f32[8,2048]{1,0:T(8,128)} %get-tuple-element.10.cos, f32[8,2048]{1,0:T(8,128)} %get-tuple-element.9.sin, f32[64,8,2048]{2,1,0:T(8,128)} %all-gather.2.cloned.1.call-done.loc, f32[512,8,128]{2,1,0:T(8,128)} %shard_map.84.child), custom_call_target="tpu_custom_call" | custom-call | tf_op jit(solution)/shard_map/pallas_call | solution.py:186
  167.7 3.1 %copy.10 = f32[128,8,512]{2,1,0:T(8,128)} copy(f32[128,8,512]{0,1,2:T(8,128)} %bitcast.5) | data formatting | bytes 4194304 | tf_op jit(solution)/shard_map/transpose | solution.py:199
  (1 shorter events, 0.0 us)
Async XLA Ops:
  6.5 79.0 %copy-start = (f32[2,32,2048]{2,1,0:T(8,128)S(1)}, f32[2,32,2048]{2,1,0:T(8,128)}, u32[]{:S(2)}) copy-start(f32[2,32,2048]{2,1,0:T(8,128)} %param.14) | copy-start | bytes 1572868
  6.5 3.2 %copy-start.2 = (f32[8,2048]{1,0:T(8,128)S(1)}, f32[8,2048]{1,0:T(8,128)}, u32[]{:S(2)}) copy-start(f32[8,2048]{1,0:T(8,128)} %param.13) | copy-start | bytes 196612
  6.5 71.8 %reduce-scatter.2.cloned.1.call-start = ((), (), s32[]{:S(2)}) async-start(), calls=%async_computation.1 | async-start | bytes 5242880 | tf_op jit(solution)/shard_map/reduce_scatter | solution.py:165
  31.0 111.6 %all-gather.2.cloned.1.call-start = ((), (), s32[]{:S(2)}) async-start(), calls=%async_computation.2 | async-start | bytes 5242880 | tf_op jit(solution)/shard_map/all_gather | solution.py:185
  79.4 14.6 %collective-permute-start = (f32[16,8,512]{2,1,0:T(8,128)S(1)}, f32[16,8,512]{2,1,0:T(8,128)S(1)}, u32[]{:S(2)}, u32[]{:S(2)}) collective-permute-start(f32[16,8,512]{2,1,0:T(8,128)S(1)} %get-tuple-element.7), channel_id=1, source_target_pairs={{0,4},{4,8},{8,12},{12,16},{16,20},{20,24},{24,28},{1,5},{5,9},{9,... | collective-permute-start | bytes 786440 | tf_op jit(solution)/shard_map/ppermute | solution.py:134
  82.8 11.2 %collective-permute-start.1 = (f32[16,8,512]{2,1,0:T(8,128)S(1)}, f32[16,8,512]{2,1,0:T(8,128)S(1)}, u32[]{:S(2)}, u32[]{:S(2)}) collective-permute-start(f32[16,8,512]{2,1,0:T(8,128)S(1)} %get-tuple-element.8), channel_id=1, source_target_pairs={{4,0},{8,4},{12,8},{16,12},{20,16},{24,20},{28,24},{5,1},{9,5},{13... | collective-permute-start | bytes 786440 | tf_op jit(solution)/shard_map/ppermute | solution.py:135
  96.5 10.5 %copy-start.1 = (f32[128,8,512]{0,1,2:T(8,128)S(1)}, f32[128,8,512]{0,1,2:T(8,128)}, u32[]{:S(2)}) copy-start(f32[128,8,512]{0,1,2:T(8,128)} %copy.9) | copy-start | bytes 6291460
  96.5 16.2 %copy-start.3 = (s32[4,512]{1,0:T(4,128)S(1)}, s32[4,512]{1,0:T(4,128)}, u32[]{:S(2)}) copy-start(s32[4,512]{1,0:T(4,128)} %param.10) | copy-start | bytes 24580
  106.9 6.3 %collective-permute-start.2 = (f32[2,8,128]{2,1,0:T(8,128)S(1)}, f32[2,8,128]{2,1,0:T(8,128)S(1)}, u32[]{:S(2)}, u32[]{:S(2)}) collective-permute-start(f32[2,8,128]{2,1,0:T(8,128)S(1)} %get-tuple-element.5), channel_id=1, source_target_pairs={{0,4},{4,8},{8,12},{12,16},{16,20},{20,24},{24,28},{1,5},{5,9},{9,... | collective-permute-start | bytes 24584 | tf_op jit(solution)/shard_map/ppermute | solution.py:134
  111.3 5.9 %collective-permute-start.3 = (f32[2,8,128]{2,1,0:T(8,128)S(1)}, f32[2,8,128]{2,1,0:T(8,128)S(1)}, u32[]{:S(2)}, u32[]{:S(2)}) collective-permute-start(f32[2,8,128]{2,1,0:T(8,128)S(1)} %get-tuple-element.6), channel_id=1, source_target_pairs={{4,0},{8,4},{12,8},{16,12},{20,16},{24,20},{28,24},{5,1},{9,5},{13... | collective-permute-start | bytes 24584 | tf_op jit(solution)/shard_map/ppermute | solution.py:135
Sparse Core Ops, SparseCore 0:
  31.1 47.1 reduce-scatter.1
  107.0 35.4 all-gather.1
where the time goes:
time: 178 us
  waiting for transfers between devices  76.2 us (43%)
  Pallas kernels  62.7 us (35%)
  between operations  13.5 us (8%)
  starting transfers between devices  10.4 us (6%)
  local copies, waits for them, and re-layouts  8.92 us (5%)
  other arithmetic  5.99 us (3%)
    reduce_scatter x1, waiting for transfers between devices, body(): field = lax.psum_scatter(field, 'dir', scatter_dimension=2, tiled=True)  47.3 us
    pallas_call x1, Pallas kernels, body(): pl.pallas_call(down_kernel, grid=(p_all // chunk,), out_shape=jax.ShapeDt...  25.1 us
    pallas_call x1, Pallas kernels, body(): pl.pallas_call(up_kernel, grid=(p_all // chunk,), out_shape=jax.ShapeDtyp...  20.3 us
    pallas_call x2, Pallas kernels, translate(): pl.pallas_call(functools.partial(translate_kernel, reach=reach), out_shap...  17.2 us
    all_gather x1, waiting for transfers between devices, body(): local = lax.all_gather(local, 'dir', axis=2, tiled=True)  17.1 us
    ppermute x2, starting transfers between devices, halo(): low = lax.ppermute(block[-width:], 'box', forward)  7.79 us
    ppermute x2, waiting for transfers between devices, halo(): low = lax.ppermute(block[-width:], 'box', forward)  7.76 us
    ppermute x2, waiting for transfers between devices, halo(): high = lax.ppermute(block[:width], 'box', backward)  4.01 us
  transfers between devices with their start and end apart: 6, of which 4 were waited for; matrix products, arithmetic and copies ran while one was open for 2% of the time, Pallas kernels for 4%

commit v1 on v0

v1 whole, which is shorter than its diff:
```python
import functools

import jax
import jax.numpy as jnp
from jax import lax
from jax.experimental import pallas as pl
from jax.experimental.pallas import tpu as pltpu
from jax.sharding import PartitionSpec as P

F32, BF16 = jnp.float32, jnp.bfloat16
VMEM_LIMIT = 60 * 1024 * 1024
MESH = pl.DeviceIdType.MESH


def split(x):
    hi = x.astype(BF16)
    return hi, (x - hi.astype(F32)).astype(BF16)


def turn(x):
    half = x.shape[1] // 2
    return jnp.concatenate([-x[:, half:], x[:, :half]], axis=1)


def nn(a, b):
    return lax.dot_general(a, b, (((1,), (0,)), ((), ())), preferred_element_type=F32)


def nt(a, b):
    return lax.dot_general(a, b, (((1,), (1,)), ((), ())), preferred_element_type=F32)


def translate(field, at, coef, mask, put, s0, count, reach, block=4):
    comps = field(0).shape[0]
    half = comps // 2
    offsets = list(range(-reach, 0)) + list(range(1, reach + 1))

    def step(i, _):
        s = s0 + i * block
        real = [jnp.zeros((comps, 128), F32) for _ in range(block)]
        imag = [jnp.zeros((comps, 128), F32) for _ in range(block)]
        for k, t in enumerate(offsets):
            cr, ci = coef(0, k), coef(1, k)
            for j in range(block):
                f = field(at + s + j + t) * mask(k, s + j)
                real[j] = real[j] + f * cr
                imag[j] = imag[j] + f * ci
        for j in range(block):
            b = imag[j]
            put(s + j, real[j] + jnp.concatenate([-b[half:], b[:half]], axis=0))
        return 0

    lax.fori_loop(0, count // block, step, 0)


def kernel(
    idx, wgt, cos, sin, child_coef, coef, child_mask, mask, pat,
    out,
    cbuf, xhi, xlo, whi, wlo, part, crecv, xsend, xrecv, field, gl, acc,
    local_sem, ch_send, ch_recv, core_send, core_recv, x_send, x_recv, halo_send, halo_recv,
    lx_send, lx_recv, lc_send, lc_recv, fw_send, fw_recv,
):
    n_chunk, n_x = whi.shape[0], whi.shape[1]
    boxes, comps, q = pat.shape
    group = cos.shape[0]
    s_count = boxes // group
    rows = s_count * comps
    p_all = idx.shape[1]
    p_own = p_all // (n_x * 2)
    sub = p_own // n_chunk
    n = group * q
    c_reach = child_coef.shape[1] // 2
    reach = coef.shape[1] // 2
    me = lax.axis_index("dir")
    box = lax.axis_index("box")
    n_box = lax.axis_size("box")
    x, core = me // 2, me % 2
    mate = 2 * x + 1 - core
    across = 2 * (1 - x) + core
    has_low, has_high = box > 0, box < n_box - 1

    def remote(src, dst, send, recv, to):
        return pltpu.make_async_remote_copy(
            src_ref=src, dst_ref=dst, send_sem=send, recv_sem=recv, device_id=to, device_id_type=MESH
        )

    load = pltpu.make_async_copy(pat, cbuf.at[pl.ds(c_reach, boxes)], local_sem)
    load.start()

    barrier = pltpu.get_barrier_semaphore()
    pl.semaphore_signal(barrier, inc=1, device_id={"dir": mate}, device_id_type=MESH)
    pl.semaphore_signal(barrier, inc=1, device_id={"dir": across}, device_id_type=MESH)

    @pl.when(has_low)
    def _():
        pl.semaphore_signal(barrier, inc=1, device_id={"box": box - 1}, device_id_type=MESH)

    @pl.when(has_high)
    def _():
        pl.semaphore_signal(barrier, inc=1, device_id={"box": box + 1}, device_id_type=MESH)

    pl.semaphore_wait(barrier, 2 + has_low.astype(jnp.int32) + has_high.astype(jnp.int32))

    def child_down():
        return remote(cbuf.at[pl.ds(c_reach, c_reach)], cbuf.at[pl.ds(c_reach + boxes, c_reach)],
                      ch_send.at[0], ch_recv.at[0], {"box": box - 1})

    def child_up():
        return remote(cbuf.at[pl.ds(boxes, c_reach)], cbuf.at[pl.ds(0, c_reach)],
                      ch_send.at[1], ch_recv.at[1], {"box": box + 1})

    def core_copy(j, a):
        return remote(part.at[j, 2 * a + 1 - core], crecv.at[j, a],
                      core_send.at[j, a], core_recv.at[j, a], {"dir": mate})

    def x_copy(j):
        return remote(xsend.at[j], xrecv.at[j], x_send.at[j], x_recv.at[j], {"dir": across})

    def halo_down(j):
        return remote(field.at[j, pl.ds(reach, reach)], field.at[j, pl.ds(reach + s_count, reach)],
                      halo_send.at[j, 0], halo_recv.at[j, 0], {"box": box - 1})

    def halo_up(j):
        return remote(field.at[j, pl.ds(s_count, reach)], field.at[j, pl.ds(0, reach)],
                      halo_send.at[j, 1], halo_recv.at[j, 1], {"box": box + 1})

    def local_x(j):
        return remote(gl.at[j, me], gl.at[j, me], lx_send.at[j], lx_recv.at[j], {"dir": across})

    def local_core(j):
        return remote(gl.at[j, me], gl.at[j, me], lc_send.at[j], lc_recv.at[j], {"dir": mate})

    def forward(j):
        return remote(gl.at[j, across], gl.at[j, across], fw_send.at[j], fw_recv.at[j], {"dir": mate})

    load.wait()

    @pl.when(has_low)
    def _():
        child_down().start()

    @pl.when(has_high)
    def _():
        child_up().start()

    for g in range(group):
        y = cbuf[c_reach : c_reach + boxes].reshape(s_count, group, comps, q)[:, g]
        for part_no, z in enumerate((y, turn(y))):
            hi, lo = split(z.reshape(rows, q))
            at = (part_no * group + g) * q
            xhi[:, at : at + q] = hi
            xlo[:, at : at + q] = lo

    first = me * q

    def send_x(j):
        for a in range(n_x):
            core_copy(j, a).wait_recv()
        xsend[j] = part[j, across] + crecv[j, 1 - x]
        x_copy(j).start()

    def upward(j, _):
        def half(a, _):
            for c in range(2):
                cols = pl.ds(pl.multiple_of((2 * a + c) * p_own + j * sub, sub), sub)
                row_no = first + lax.broadcasted_iota(jnp.int32, (q, sub), 0)
                m = jnp.zeros((q, sub), F32)
                for k in range(idx.shape[0]):
                    m = m + jnp.where(row_no == idx[k : k + 1, cols], wgt[k : k + 1, cols], F32(0.0))
                for part_no, table in enumerate((cos, sin)):
                    for g in range(group):
                        hi, lo = split(m * table[g : g + 1, cols])
                        at = (part_no * group + g) * q
                        whi[j, a, at : at + q, c * sub : (c + 1) * sub] = hi
                        wlo[j, a, at : at + q, c * sub : (c + 1) * sub] = lo
            total = nn(xhi[...], whi[j, a]) + nn(xhi[...], wlo[j, a]) + nn(xlo[...], whi[j, a])
            for c in range(2):
                part[j, 2 * a + c] = total[:, c * sub : (c + 1) * sub].reshape(s_count, comps, sub)
            core_copy(j, a).start()
            return 0

        lax.fori_loop(0, n_x, half, 0)

        @pl.when(j > 0)
        def _():
            send_x(j - 1)

        return 0

    lax.fori_loop(0, n_chunk, upward, 0)
    send_x(n_chunk - 1)

    @pl.when(jnp.logical_not(has_low))
    def _():
        cbuf[0:c_reach] = jnp.zeros((c_reach, comps, q), F32)
        for j in range(n_chunk):
            field[j, 0:reach] = jnp.zeros((reach, comps, sub), F32)

    @pl.when(jnp.logical_not(has_high))
    def _():
        cbuf[c_reach + boxes :] = jnp.zeros((c_reach, comps, q), F32)
        for j in range(n_chunk):
            field[j, reach + s_count :] = jnp.zeros((reach, comps, sub), F32)

    @pl.when(has_low)
    def _():
        child_up().wait_recv()

    @pl.when(has_high)
    def _():
        child_down().wait_recv()

    quarter = boxes // n_chunk

    def middle(j, _):
        @pl.when(j < n_chunk)
        def _():
            x_copy(j).wait_recv()
            field[j, reach : reach + s_count] = part[j, me] + crecv[j, x] + xrecv[j]

            @pl.when(has_low)
            def _():
                halo_down(j).start()

            @pl.when(has_high)
            def _():
                halo_up(j).start()

            def put(s, v):
                out[s] = v

            translate(
                lambda i: cbuf[i], c_reach, lambda r, k: child_coef[r, k : k + 1, :],
                lambda k, s: child_mask[k, s], put, j * quarter, quarter, c_reach,
            )

        @pl.when(j > 0)
        def _():
            i = j - 1

            @pl.when(has_low)
            def _():
                halo_up(i).wait_recv()

            @pl.when(has_high)
            def _():
                halo_down(i).wait_recv()

            def put(s, v):
                gl[i, me, s] = v

            cols = pl.ds(pl.multiple_of(i * sub, sub), sub)
            translate(
                lambda s: field[i, s], reach, lambda r, k: coef[r, k : k + 1, cols],
                lambda k, s: mask[k, s], put, 0, s_count, reach,
            )
            local_x(i).start()
            local_core(i).start()

        @pl.when(j > 1)
        def _():
            local_x(j - 2).wait_recv()
            forward(j - 2).start()

        return 0

    lax.fori_loop(0, n_chunk + 1, middle, 0)

    def downward(j, _):
        @pl.when(j == 1)
        def _():
            local_x(n_chunk - 1).wait_recv()
            forward(n_chunk - 1).start()

        local_core(j).wait_recv()
        forward(j).wait_recv()
        total = None
        for a in range(n_x):
            y = [gl[j, 2 * a + c] for c in range(2)]
            for part_no in range(2):
                z = y if part_no == 0 else [-turn(v) for v in y]
                hi, lo = split(jnp.concatenate([v.reshape(rows, sub) for v in z], axis=1))
                wh = whi[j, a, part_no * n : (part_no + 1) * n, :]
                wl = wlo[j, a, part_no * n : (part_no + 1) * n, :]
                for term in (nt(hi, wh), nt(hi, wl), nt(lo, wh)):
                    total = term if total is None else total + term

        @pl.when(j == 0)
        def _():
            acc[...] = total

        @pl.when(j > 0)
        def _():
            acc[...] = acc[...] + total

        return 0

    lax.fori_loop(0, n_chunk, downward, 0)

    def put_out(s, _):
        at = pl.ds(pl.multiple_of(s * comps, comps), comps)
        for g in range(group):
            out[s * group + g] = out[s * group + g] + acc[at, g * q : (g + 1) * q]
        return 0

    lax.fori_loop(0, s_count, put_out, 0)

    def finish(j, _):
        for a in range(n_x):
            core_copy(j, a).wait_send()
        x_copy(j).wait_send()
        local_x(j).wait_send()
        local_core(j).wait_send()
        forward(j).wait_send()

        @pl.when(has_low)
        def _():
            halo_down(j).wait_send()

        @pl.when(has_high)
        def _():
            halo_up(j).wait_send()

        return 0

    lax.fori_loop(0, n_chunk, finish, 0)

    @pl.when(has_low)
    def _():
        child_down().wait_send()

    @pl.when(has_high)
    def _():
        child_up().wait_send()


def body(pattern, child_coef, child_mask, interp_index, interp_weight, phase_angle, parent_coef, parent_mask):
    q, comps, boxes = pattern.shape
    p_all = interp_index.shape[1]
    group = phase_angle.shape[0]
    s_count = boxes // group
    n_x = lax.axis_size("dir") // 2
    p_own = p_all // (2 * n_x)
    sub = 128
    n_chunk = p_own // sub
    rows, wsize = s_count * comps, 2 * group * q
    c_reach = child_coef.shape[1] // 2
    reach = parent_coef.shape[1] // 2
    dir_rank = lax.axis_index("dir")
    box_rank = lax.axis_index("box")
    cos, sin = jnp.cos(phase_angle), jnp.sin(phase_angle)
    pat = jnp.transpose(pattern, (2, 1, 0))
    own_coef = lax.dynamic_slice_in_dim(parent_coef, dir_rank * p_own, p_own, 2)
    own_mask = lax.dynamic_slice_in_dim(parent_mask, box_rank * s_count, s_count, 1).astype(F32)
    vmem = pl.BlockSpec(memory_space=pltpu.VMEM)
    smem = pl.BlockSpec(memory_space=pltpu.SMEM)
    dma = pltpu.SemaphoreType.DMA
    block = (s_count, comps, sub)
    out = pl.pallas_call(
        kernel,
        out_shape=jax.ShapeDtypeStruct((boxes, comps, q), F32),
        in_specs=[vmem] * 6 + [smem] * 2 + [pl.BlockSpec(memory_space=pl.ANY)],
        out_specs=vmem,
        scratch_shapes=[
            pltpu.VMEM((boxes + 2 * c_reach, comps, q), F32),
            pltpu.VMEM((rows, wsize), BF16),
            pltpu.VMEM((rows, wsize), BF16),
            pltpu.VMEM((n_chunk, n_x, wsize, 2 * sub), BF16),
            pltpu.VMEM((n_chunk, n_x, wsize, 2 * sub), BF16),
            pltpu.VMEM((n_chunk, 2 * n_x) + block, F32),
            pltpu.VMEM((n_chunk, n_x) + block, F32),
            pltpu.VMEM((n_chunk,) + block, F32),
            pltpu.VMEM((n_chunk,) + block, F32),
            pltpu.VMEM((n_chunk, s_count + 2 * reach, comps, sub), F32),
            pltpu.VMEM((n_chunk, 2 * n_x) + block, F32),
            pltpu.VMEM((rows, group * q), F32),
            dma(()), dma((2,)), dma((2,)),
            dma((n_chunk, n_x)), dma((n_chunk, n_x)),
            dma((n_chunk,)), dma((n_chunk,)),
            dma((n_chunk, 2)), dma((n_chunk, 2)),
        ] + [dma((n_chunk,))] * 6,
        compiler_params=pltpu.CompilerParams(
            vmem_limit_bytes=VMEM_LIMIT, collective_id=0, has_side_effects=True
        ),
    )(interp_index, interp_weight, cos, sin, child_coef, own_coef, child_mask.astype(F32), own_mask, pat)
    return jnp.transpose(out, (2, 1, 0))


def solution(mesh):
    placed = (P("dir", None, "box"), P(None, None, "dir"), P(None, "box"), P(), P(), P(), P(), P())
    return jax.shard_map(
        body, mesh=mesh, in_specs=placed, out_specs=P("dir", None, "box"), check_vma=False
    )
```

time: 178 us -> 86.6 us (0.49)
  waiting for transfers between devices: 76.2 us -> 0 us
  between operations: 13.5 us -> 0.01 us
  Pallas kernels: 62.7 us -> 75 us
  starting transfers between devices: 10.4 us -> 0 us
  other arithmetic: 5.99 us -> 2.73 us
    reduce_scatter x1 -> x0, waiting for transfers between devices: 47.3 us -> none  [body(): field = lax.psum_scatter(field, 'dir', scatter_dimension=2, tiled=True)]
    all_gather x1 -> x0, waiting for transfers between devices: 17.1 us -> none  [body(): local = lax.all_gather(local, 'dir', axis=2, tiled=True)]
    pallas_call x4 -> x1, Pallas kernels: 62.7 us -> 75 us  [body(): pl.pallas_call(kernel, out_shape=jax.ShapeDtypeStruct((boxes, comps, q),...]
    ppermute x4 -> x0, waiting for transfers between devices: 11.8 us -> none  [the longest x2 7.76 us: halo(): low = lax.ppermute(block[-width:], 'box', forward)]
    ppermute x4 -> x0, starting transfers between devices: 10.4 us -> none  [the longest x2 7.79 us: halo(): low = lax.ppermute(block[-width:], 'box', forward)]
    concatenate x2 -> x0, other arithmetic: 4 us -> none  [halo(): return jnp.concatenate([low, block, high], axis=0)]
  transfers between devices with their start and end apart: 6 -> 0, of which waited for: 4 -> 0; matrix products, arithmetic and copies ran while one was open for 2% -> 0% of each run, Pallas kernels for 4% -> 0%
where the time goes in v1:
time: 86.6 us; the launch traced here: 86.3 us
  Pallas kernels  75 us (87%)
  local copies, waits for them, and re-layouts  8.61 us (10%)
  other arithmetic  2.73 us (3%)
    pallas_call x1, Pallas kernels, body(): pl.pallas_call(kernel, out_shape=jax.ShapeDtypeStruct((boxes, comps, q),...  75 us
    transpose x1, local copies, waits for them, and re-layouts, body(): return jnp.transpose(out, (2, 1, 0))  3.11 us
    unnamed x3, local copies, waits for them, and re-layouts  3.09 us
    sin x1, local copies, waits for them, and re-layouts, body(): cos, sin = (jnp.cos(phase_angle), jnp.sin(phase_angle))  1.73 us

profile of v1, /device:TPU:0, one launch (start us, length us, event | category | flops | bytes accessed | tf_op | source)
XLA Modules:
  0.0 86.3 jit_solution(6317444767179563021)
XLA Ops:
  0.0 0.0 copy-start
  0.0 1.3 %convert_element_type.6.child_mask = f32[4,512]{1,0:T(4,128)} convert(s32[4,512]{1,0:T(4,128)} %param.10) | non-fusion elementwise | flops 2048 | bytes 16384 | tf_op jit(solution)/shard_map/convert_element_type | solution.py:385
  1.3 1.4 %dynamic-slice_convert_fusion.mask = f32[32,64]{1,0:T(8,128)} fusion(s32[32,512]{1,0:T(8,128)} %param.15, s32[]{:T(128)S(6)} %select_n.7), kind=kLoop, calls=%fused_computation | loop fusion | flops 2048 | bytes 16388 | tf_op jit(solution)/shard_map/convert_element_type | solution.py:354
  2.7 0.0 copy-done
  2.7 0.7 constant_dynamic-slice_fusion.coef
  3.4 1.7 %fusion = (f32[8,2048]{1,0:T(8,128)}, f32[8,2048]{1,0:T(8,128)}) fusion(f32[8,2048]{1,0:T(8,128)} %param.13), kind=kLoop, calls=%fused_computation.2 | loop fusion | bytes 196608 | tf_op jit(solution)/shard_map/sin | solution.py:351
  5.1 3.1 %copy.9 = f32[128,8,512]{0,1,2:T(8,128)} copy(f32[128,8,512]{2,1,0:T(8,128)} %param.8) | data formatting | bytes 4194304 | tf_op args[0]
  8.2 75.0 %shard_map.82 = f32[512,8,128]{2,1,0:T(8,128)} custom-call(s32[16,2048]{1,0:T(8,128)} %idx.1, f32[16,2048]{1,0:T(8,128)} %wgt.1, f32[8,2048]{1,0:T(8,128)} %get-tuple-element.6.cos, f32[8,2048]{1,0:T(8,128)} %get-tuple-element.5.sin, f32[2,4,128]{2,1,0:T(4,128)} %child_coef.1, f32[2,32,512]{2,1,0:T(8,128)} %constant_dynamic-slice_fusion.coef, ...), custom_call_target="tpu_custom_call" | custom-call | tf_op jit(solution)/shard_map/pallas_call | solution.py:359
  83.2 3.1 %copy.10 = f32[128,8,512]{2,1,0:T(8,128)} copy(f32[128,8,512]{0,1,2:T(8,128)} %bitcast.2) | data formatting | bytes 4194304 | tf_op jit(solution)/shard_map/transpose | solution.py:386
Async XLA Ops:
  0.0 2.7 %copy-start = (f32[2,32,2048]{2,1,0:T(8,128)S(1)}, f32[2,32,2048]{2,1,0:T(8,128)}, u32[]{:S(2)}) copy-start(f32[2,32,2048]{2,1,0:T(8,128)} %param.14) | copy-start | bytes 1572868
